TPU v7x, 32 devices: a whole 2x2x4 slice. The times are simulated.
32 devices in a mesh: groups: 2 (over y), dp: 16 (over z, x, core).
Axes of the slice: x: 2, y: 2, z: 4, core: 2. Of those that a mesh axis runs over, the one named last changes fastest.
Arguments:
- query_states: bfloat16 [128, 128, 2048], P(('groups', 'dp')), parts along dimension 0, may hold values from -4.5 to 4.5
- key_states: bfloat16 [128, 128, 512], P(('groups', 'dp')), parts along dimension 0, may hold values from -4.5 to 4.5
- value_states: bfloat16 [128, 128, 512], P(('groups', 'dp')), parts along dimension 0, may hold values from -56 to 56
- out_weight: bfloat16 [2048, 2048], P('dp'), may hold values from -0.125 to 0.125
- token_ids: int32 [128, 128], P(('groups', 'dp')), parts along dimension 0, may hold values from 0 to 31999, as said below
- keep_flags: int32 [128], P(('groups', 'dp')), parts along dimension 0, may hold values from 0 to 1, as said below
- list_ids: int32 [128, 128], P(('groups', 'dp')), parts along dimension 0, may hold values from 0 to 1023, as said below
- owner_map: int32 [2048], P('groups'), parts along dimension 0, may hold values from 0 to 15, as said below
Outputs:
- doc_vectors: bfloat16 [96, 2048], P(('groups', 'dp')), parts along dimension 0
- token_vectors: bfloat16 [16384, 2048], P(('groups', 'dp')), parts along dimension 0
- token_keys: int32 [16384], P(('groups', 'dp')), parts along dimension 0
There are 2 independent parts, one for each index of `groups`. A program takes and returns all parts, laid end to end along the dimension named above; an argument that names none is the same for every part. Nothing has to cross between parts.
Inputs may be any that keep to these rules, and one draw needn't show every extreme that they name: `token_ids`: in each document the ids are 0 exactly from its length on, and its length lies between 96 and 128. `keep_flags`: exactly 48 documents have the flag 1. `list_ids`: the tokens of the 4 documents of one index of dp name lists of any one owner between 16 and 48 times, exactly 48 times for some owner; over all 64 documents the lists of each owner are named exactly 512 times. `owner_map`: every owner holds exactly 64 lists.
All inputs are finite; a program needn't handle non-finite values.
Results may differ from a plain program's by a relative error of at most 0.0057.
Values may be sent and summed in bfloat16 or wider, within the bound.
A program may use at most 64 MiB of HBM per device.

v0:
```python
import math
import jax
import jax.numpy as jnp
from jax import lax
from jax.sharding import PartitionSpec as P

HEAD_DIM = 128


def carried_in(part, axis, combine, identity):
    place = lax.axis_index(axis)
    gathered = lax.all_gather(part, axis)
    state = jnp.zeros_like(part) + jnp.asarray(identity, part.dtype)

    def one(lap, state):
        return combine(state, lax.dynamic_index_in_dim(gathered, lap, 0, False))

    return lax.fori_loop(0, place, one, state)


def add_counts(earlier, later):
    return earlier + later


def normalize(values):
    return (values * lax.rsqrt(jnp.mean(values * values, axis=-1, keepdims=True) + 1e-06)).astype(
        jnp.bfloat16
    )


def attend(query_states, key_states, value_states, token_ids):
    doc_count, length, features = query_states.shape
    kv_features = key_states.shape[2]
    kv_count = kv_features // HEAD_DIM
    group_size = features // kv_features
    queries = query_states.reshape(doc_count, length, kv_count, group_size, HEAD_DIM)
    keys_split = key_states.reshape(doc_count, length, kv_count, HEAD_DIM)
    values_split = value_states.reshape(doc_count, length, kv_count, HEAD_DIM)
    scores = jnp.einsum(
        "nqhgd,nshd->nhgqs", queries, keys_split, preferred_element_type=jnp.float32
    ) / math.sqrt(HEAD_DIM)
    present = token_ids != 0
    scores = jnp.where(present[:, None, None, None, :], scores, -jnp.inf)
    row_max = jnp.max(scores, axis=-1, keepdims=True)
    weights = jnp.exp(scores - row_max)
    weights = (weights / jnp.sum(weights, axis=-1, keepdims=True)).astype(jnp.bfloat16)
    attended = jnp.einsum(
        "nhgqs,nshd->nqhgd", weights, values_split, preferred_element_type=jnp.float32
    )
    attended = attended.reshape(doc_count, length, features).astype(jnp.bfloat16)
    counts = jnp.sum(present.astype(jnp.float32), axis=1)
    pooled_attended = (
        jnp.einsum(
            "nt,ntf->nf", present.astype(jnp.bfloat16), attended, preferred_element_type=jnp.float32
        )
        / counts[:, None]
    )
    return (attended, pooled_attended)


def project(rows, pooled_attended, out_weight):
    piece = lax.all_gather(out_weight, "dp", axis=0, tiled=True)
    row_sum = jnp.dot(rows, piece, preferred_element_type=jnp.float32)
    pooled_sum = jnp.dot(
        pooled_attended, piece.astype(jnp.float32), precision=lax.Precision.HIGHEST
    )
    return (row_sum, pooled_sum)


def send_to_owners(rows, usable, sort_keys, owners, axis_size):
    row_count, width = rows.shape
    capacity = 3 * row_count // (2 * axis_size)
    owner_index = jnp.arange(axis_size, dtype=jnp.int32)
    member = ((owners[:, None] == owner_index[None, :]) & usable[:, None]).astype(jnp.int32)
    running = jnp.cumsum(member, axis=0)
    within = jnp.take_along_axis(running, owners[:, None], axis=1)[:, 0] - 1
    slots = jnp.where(usable, owners * capacity + within, axis_size * capacity)
    packed = jnp.zeros((axis_size * capacity, width), rows.dtype).at[slots].set(rows, mode="drop")
    packed_keys = (
        jnp.full((axis_size * capacity,), -1, jnp.int32).at[slots].set(sort_keys, mode="drop")
    )
    arrived, arrived_keys = (
        lax.all_to_all(
            packed.reshape(axis_size, capacity, width),
            "dp",
            split_axis=0,
            concat_axis=0,
            tiled=True,
        ),
        lax.all_to_all(
            packed_keys.reshape(axis_size, capacity), "dp", split_axis=0, concat_axis=0, tiled=True
        ),
    )
    arrived = arrived.reshape(-1, width)
    arrived_keys = arrived_keys.reshape(-1)
    filled = arrived_keys >= 0
    smaller = jnp.sum(filled[None, :] & (arrived_keys[None, :] < arrived_keys[:, None]), axis=1)
    targets = jnp.where(filled, smaller, row_count)
    sorted_rows = jnp.zeros((row_count, width), rows.dtype).at[targets].set(arrived, mode="drop")
    sorted_keys = jnp.full((row_count,), -1, jnp.int32).at[targets].set(arrived_keys, mode="drop")
    return (sorted_rows, sorted_keys)


def shards(
    query_states, key_states, value_states, out_weight, token_ids, keep_flags, list_ids, owner_map
):
    axis_size = lax.axis_size("dp")
    my_index = lax.axis_index("dp")
    slot_count = keep_flags.shape[0]
    kept_slots = 3 * slot_count // 4
    before = carried_in(keep_flags, "dp", add_counts, jnp.zeros_like(keep_flags))
    totals = lax.psum(keep_flags.astype(jnp.float32), "dp").astype(jnp.int32)
    earlier = jnp.cumsum(totals) - totals
    occupied = keep_flags == 1
    position = (earlier + before).astype(jnp.int32)
    doc_rank = jnp.where(occupied, position, -1)
    attended, pooled_attended = attend(query_states, key_states, value_states, token_ids)
    doc_count, length, features = attended.shape
    flat_rows = attended.reshape(doc_count * length, features)
    owners = jnp.take(owner_map, list_ids, axis=0).reshape(-1)
    usable_grid = occupied[:, None] & (token_ids != 0)
    positions = jnp.arange(length, dtype=jnp.int32)
    sort_keys = jnp.where(usable_grid, doc_rank[:, None] * length + positions[None, :], -1).reshape(
        -1
    )
    usable = usable_grid.reshape(-1)
    projected, pooled = project(flat_rows, pooled_attended, out_weight)
    unit_tokens = normalize(projected)
    token_vectors, token_keys = send_to_owners(unit_tokens, usable, sort_keys, owners, axis_size)
    unit_docs = normalize(pooled)
    every_doc, every_rank = (
        lax.all_gather(unit_docs, "dp", axis=0, tiled=True),
        lax.all_gather(doc_rank, "dp", axis=0, tiled=True),
    )
    wanted = jnp.arange(kept_slots, dtype=jnp.int32) * axis_size + my_index
    picker = (every_rank[None, :] == wanted[:, None]).astype(jnp.bfloat16)
    doc_vectors = jnp.dot(picker, every_doc, preferred_element_type=jnp.float32).astype(
        jnp.bfloat16
    )
    return (doc_vectors, token_vectors, token_keys)


def solution(mesh):
    return jax.shard_map(
        shards,
        mesh=mesh,
        in_specs=(
            P(("groups", "dp"), None, None),
            P(("groups", "dp"), None, None),
            P(("groups", "dp"), None, None),
            P("dp", None),
            P(("groups", "dp"), None),
            P(("groups", "dp")),
            P(("groups", "dp"), None),
            P("groups"),
        ),
        out_specs=(P(("groups", "dp"), None), P(("groups", "dp"), None), P(("groups", "dp"))),
        check_vma=False,
    )
```

profile of v0, /device:TPU:0, one launch (start us, length us, event | category | flops | bytes accessed | tf_op | source)
XLA Modules:
  0.0 237.1 jit_solution(729401904148163551)
XLA Ops:
  7.2 0.7 all-gather.4.cloned.1.call-update
  8.6 35.5 %psum.7 = f32[4]{0:T(128)S(1)} all-reduce(f32[4]{0:T(128)S(1)} %convert_element_type.46), channel_id=1, replica_groups=mesh['groups'=2,'dp'=16] {'dp'}, use_global_device_ids=true, to_apply=%region_0.1 | all-reduce | flops 4 | bytes 32 | tf_op jit(solution)/shard_map/psum | solution.py:112
  44.1 1.2 dynamic-slice
  46.0 0.9 dynamic-update-slice
  46.9 8.3 %all-reduce = s32[64]{0:T(128)S(1)} all-reduce(s32[64]{0:T(128)S(1)} %dynamic-update-slice), channel_id=2, replica_groups=mesh['groups'=2,'dp'=16] {'dp'}, use_global_device_ids=true, to_apply=%add | all-reduce | flops 64 | bytes 512
  55.4 0.7 fusion.35
  56.1 2.3 gather_fusion
  58.4 0.7 broadcast_compare_fusion.2
  59.8 0.8 select_bitcast_fusion
  60.5 0.7 bitcast_select_fusion.1
  61.2 1.2 reduce-window.20
  62.8 4.5 %gather_fusion.1 = s32[512]{0:T(512)S(1)} fusion(s32[512,16]{0,1:T(8,128)S(1)} %bitcast_bitcast_fusion, s32[512]{0:T(512)S(1)} %bitcast.79), kind=kCustom, calls=%fused_computation.1 | custom fusion | bytes 8192 | tf_op jit(solution)/shard_map/jit(take_along_axis)/gather | solution.py:76
  67.3 2.4 %scatter_custom_fusion = s32[768]{0:T(1024)S(1)} fusion(s32[512]{0:T(512)S(1)} %bitcast.89, s32[512]{0:T(512)S(1)} %get-tuple-element.35, s32[]{:T(128)} %constant.29.clone.1), kind=kCustom, calls=%fused_computation.67 | custom fusion | bytes 3076 | tf_op jit(solution)/shard_map/scatter | solution.py:80
  69.8 0.7 all_to_all.9
  70.5 6.3 %all-to-all-start = ((s32[16,1,48]{2,1,0:T(1,128)}), s32[16,1,48]{2,1,0:T(1,128)S(1)}, u32[]{:S(2)}, u32[]{:S(2)}) async-start(s32[16,1,48]{2,1,0:T(1,128)} %all_to_all.9), calls=%async_computation | async-start | bytes 16384 | tf_op jit(solution)/shard_map/all_to_all | solution.py:90
  76.8 1.0 copy.40
  77.8 3.3 %reshape.386 = bf16[4,128,4,4,128]{4,3,2,1,0:T(4,128)(2,1)S(1)} reshape(bf16[4,128,2048]{2,1,0:T(8,128)(2,1)} %param.10) | data formatting | bytes 4194304 | tf_op jit(solution)/shard_map/reshape | solution.py:36
  81.2 0.7 fusion.6
  82.0 1.7 fusion.45
  83.7 0.7 fusion.13
  84.4 2.9 %copy.32 = bf16[4,128,4,4,128]{4,3,2,1,0:T(4,128)(2,1)} copy(bf16[4,128,4,4,128]{1,4,3,2,0:T(8,128)(2,1)S(1)} %bitcast.80) | data formatting | bytes 4194304 | tf_op jit(solution)/shard_map/convert_element_type | solution.py:50
  87.3 4.5 %convert_element_type.57 = bf16[512,2048]{1,0:T(8,128)(2,1)} reshape(bf16[4,128,4,4,128]{4,3,2,1,0:T(4,128)(2,1)} %copy.32) | data formatting | bytes 4194304 | tf_op jit(solution)/shard_map/convert_element_type | solution.py:50
  91.8 10.5 %multiply_reduce_fusion = (f32[512]{0:T(512)S(1)}, f32[512,2048]{1,0:T(8,128)}) fusion(bf16[512,2048]{1,0:T(8,128)(2,1)} %convert_element_type.57, bf16[2048,2048]{1,0:T(8,128)(2,1)} %all-gather.4.cloned.1.call-done), kind=kOutput, calls=%fused_computation.13 | convolution fusion | flops 4297063936 | bytes 14682112 | tf_op jit(solution)/shard_map/dot_general | solution.py:63
  102.3 7.4 %scatter_custom_fusion.1 = bf16[768,2048]{1,0:T(8,128)(2,1)} fusion(s32[512]{0:T(512)S(1)} %bitcast.90, f32[512,2048]{1,0:T(8,128)} %get-tuple-element.45, f32[512]{0:T(512)S(1)} %add_rsqrt_fusion, bf16[]{:T(256)} %constant.40.clone.1), kind=kCustom, calls=%fused_computation.18 | custom fusion | flops 2097152 | bytes 7342082 | tf_op jit(solution)/shard_map/scatter | solution.py:78
  109.7 6.0 %all-to-all-start.1 = ((bf16[16,48,2048]{2,1,0:T(8,128)(2,1)}), bf16[16,48,2048]{2,1,0:T(8,128)(2,1)}, u32[]{:S(2)}, u32[]{:S(2)}) async-start(bf16[16,48,2048]{2,1,0:T(8,128)(2,1)} %bitcast.24), calls=%async_computation.1 | async-start | bytes 6291456 | tf_op jit(solution)/shard_map/all_to_all | solution.py:83
  115.9 71.5 %all-reduce.1 = s32[64]{0:T(128)S(1)} all-reduce(s32[64]{0:T(128)S(1)} %dynamic-update-slice.1), channel_id=1, replica_groups=mesh['groups'=2,'dp'=16] {'dp'}, use_global_device_ids=true, to_apply=%add.1 | all-reduce | flops 64 | bytes 512
  188.8 0.7 reduce.9
  190.1 3.9 %scatter_custom_fusion.3 = s32[512]{0:T(512)} fusion(s32[768]{0:T(1024)S(1)} %fusion.28, s32[768]{0:T(1024)S(1)} %reshape.438, s32[]{:T(128)} %constant.29.clone.1), kind=kCustom, calls=%fused_computation.72 | custom fusion | bytes 2052 | tf_op jit(solution)/shard_map/scatter | solution.py:100
  194.0 5.9 %multiply_reduce_fusion.1 = (f32[4]{0:T(128)S(1)}, f32[4,2048]{1,0:T(4,128)S(1)}) fusion(bf16[2048,2048]{1,0:T(8,128)(2,1)} %all-gather.4.cloned.1.call-done, f32[4,1,2048]{2,1,0:T(1,128)S(1)} %fusion.26, f32[4]{0:T(128)S(1)} %convert_reduce_fusion.1), kind=kOutput, calls=%fused_computation.40 | convolution fusion | flops 201351168 | bytes 8454176 | tf_op jit(solution)/shard_map/dot_general | solution.py:64
  200.0 20.1 %all-gather.1 = bf16[16,4,2048]{2,1,0:T(4,128)(2,1)S(1)} all-gather(bf16[1,4,2048]{2,1,0:T(4,128)(2,1)S(1)} %fusion.24), channel_id=1, replica_groups=mesh['groups'=2,'dp'=16] {'dp'}, dimensions={0}, use_global_device_ids=true | all-gather | bytes 278528 | tf_op jit(solution)/shard_map/all_gather | solution.py:132
  220.1 0.8 convolution_convert_fusion
  220.9 9.3 %scatter_custom_fusion.2 = bf16[512,2048]{1,0:T(8,128)(2,1)} fusion(s32[768]{0:T(1024)S(1)} %fusion.28, bf16[768,2048]{1,0:T(8,128)(2,1)} %bitcast.25, bf16[]{:T(256)} %constant.40.clone.1), kind=kCustom, calls=%fused_computation.28 | custom fusion | bytes 2097664 | tf_op jit(solution)/shard_map/scatter | solution.py:99
  (48 shorter events, 4.6 us)
Async XLA Ops:
  7.2 49.0 %copy-start = (s32[1024]{0:T(1024)S(1)}, s32[1024]{0:T(1024)}, u32[]{:S(2)}) copy-start(s32[1024]{0:T(1024)} %param.17) | copy-start | bytes 12292
  7.2 69.6 %copy-start.1 = (bf16[4,128,512]{2,1,0:T(8,128)(2,1)S(1)}, bf16[4,128,512]{2,1,0:T(8,128)(2,1)}, u32[]{:S(2)}) copy-start(bf16[4,128,512]{2,1,0:T(8,128)(2,1)} %param.12) | copy-start | bytes 1572868
  7.2 84.6 %all-gather.4.cloned.1.call-start = ((), (), s32[]{:S(2)}) async-start(), calls=%async_computation.2 | async-start | bytes 8912896 | tf_op jit(solution)/shard_map/all_gather | solution.py:62
  67.3 13.8 %copy-start.2 = (bf16[4,128,512]{2,1,0:T(8,128)(2,1)S(1)}, bf16[4,128,512]{2,1,0:T(8,128)(2,1)}, u32[]{:S(2)}) copy-start(bf16[4,128,512]{2,1,0:T(8,128)(2,1)} %param.11) | copy-start | bytes 1572868
  70.5 39.2 %all-to-all-start = ((s32[16,1,48]{2,1,0:T(1,128)}), s32[16,1,48]{2,1,0:T(1,128)S(1)}, u32[]{:S(2)}, u32[]{:S(2)}) async-start(s32[16,1,48]{2,1,0:T(1,128)} %all_to_all.9), calls=%async_computation | async-start | bytes 16384 | tf_op jit(solution)/shard_map/all_to_all | solution.py:90
  82.0 1.7 copy-start.3
  109.7 111.2 %all-to-all-start.1 = ((bf16[16,48,2048]{2,1,0:T(8,128)(2,1)}), bf16[16,48,2048]{2,1,0:T(8,128)(2,1)}, u32[]{:S(2)}, u32[]{:S(2)}) async-start(bf16[16,48,2048]{2,1,0:T(8,128)(2,1)} %bitcast.24), calls=%async_computation.1 | async-start | bytes 6291456 | tf_op jit(solution)/shard_map/all_to_all | solution.py:83
Sparse Core Ops, SparseCore 0:
  10.2 78.0 all-gather.3
where the time goes:
time: 238 us; the launch traced here: 237 us
  blocking collectives  135 us (57%)
  local copies, waits for them, and re-layouts  38.4 us (16%)
  matrix products  19.2 us (8%)
  other arithmetic  16.1 us (7%)
  between operations  14.9 us (6%)
  starting transfers between devices  12.3 us (5%)
    unnamed x2, blocking collectives  79.8 us
    psum x1, blocking collectives, shards(): totals = lax.psum(keep_flags.astype(jnp.float32), 'dp').astype(jnp.int32)  35.5 us
    all_gather x1, blocking collectives, shards(): lax.all_gather(unit_docs, 'dp', axis=0, tiled=True)  20.1 us
    dot_general x1, matrix products, project(): row_sum = jnp.dot(rows, piece, preferred_element_type=jnp.float32)  10.5 us
    scatter x1, local copies, waits for them, and re-layouts, send_to_owners(): jnp.zeros((row_count, width), rows.dtype).at[targets]  9.31 us
    convert_element_type x2, local copies, waits for them, and re-layouts, attend(): attended.reshape(doc_count, length, features).astype(jnp.bfloat16)  7.39 us
    scatter x1, other arithmetic, send_to_owners(): jnp.zeros((axis_size * capacity, width), rows.dtype).at[slots]  7.38 us
    all_to_all x1, starting transfers between devices, send_to_owners(): lax.all_to_all(packed_keys.reshape(axis_size, capacity), 'dp', split_axis...  6.32 us
  transfers between devices with their start and end apart: 3, of which 0 were waited for; matrix products, arithmetic and copies ran while one was open for 27% of the time, Pallas kernels for 0%

commit v1 on v0

--- a/solution.py
+++ b/solution.py
@@ -5,6 +5,23 @@
 from jax.sharding import PartitionSpec as P
 
 HEAD_DIM = 128
+
+
+def joined_along(blocks, dim):
+    lengths = list(blocks.shape[1:])
+    lengths[dim] *= blocks.shape[0]
+    return jnp.moveaxis(blocks, 0, dim).reshape(lengths)
+
+
+def collect(value, axis, dim):
+    size = lax.axis_size(axis)
+    right = [(i, (i + 1) % size) for i in range(size)]
+    blocks = [value]
+    while len(blocks) < size:
+        blocks.append(lax.ppermute(blocks[-1], axis, right))
+    index = lax.axis_index(axis)
+    blocks = jnp.stack(blocks)[(index - jnp.arange(size)) % size]
+    return joined_along(blocks, dim)
 
 
 def carried_in(part, axis, combine, identity):
@@ -129,7 +146,7 @@
     token_vectors, token_keys = send_to_owners(unit_tokens, usable, sort_keys, owners, axis_size)
     unit_docs = normalize(pooled)
     every_doc, every_rank = (
-        lax.all_gather(unit_docs, "dp", axis=0, tiled=True),
+        collect(unit_docs, "dp", 0),
         lax.all_gather(doc_rank, "dp", axis=0, tiled=True),
     )
     wanted = jnp.arange(kept_slots, dtype=jnp.int32) * axis_size + my_index

time: 238 us -> 290 us (1.22)
  waiting for transfers between devices: 0.69 us -> 125 us
  blocking collectives: 135 us -> 56.1 us
  local copies, waits for them, and re-layouts: 38.4 us -> 47.8 us
    ppermute x0 -> x15, waiting for transfers between devices: none -> 124 us  [collect(): blocks.append(lax.ppermute(blocks[-1], axis, right))]
    unnamed x2, blocking collectives: 79.8 us -> 20.6 us
    all_gather x1 -> x0, blocking collectives: 20.1 us -> none  [shards(): lax.all_gather(unit_docs, 'dp', axis=0, tiled=True)]
    unnamed x15 -> x30, local copies, waits for them, and re-layouts: 2.45 us -> 11 us
    dot_general x1, matrix products: 10.5 us -> 6.14 us  [project(): row_sum = jnp.dot(rows, piece, preferred_element_type=jnp.float32)]
  transfers between devices with their start and end apart: 3 -> 18, of which waited for: 0 -> 14; matrix products, arithmetic and copies ran while one was open for 27% -> 22% of each run, Pallas kernels for 0% -> 0%
where the time goes in v1:
time: 290 us; the launch traced here: 289 us
  waiting for transfers between devices  125 us (43%)
  blocking collectives  56.1 us (19%)
  local copies, waits for them, and re-layouts  47.8 us (16%)
  other arithmetic  16.8 us (6%)
  matrix products  16.6 us (6%)
  between operations  15 us (5%)
  starting transfers between devices  12.6 us (4%)
    ppermute x15, waiting for transfers between devices, collect(): blocks.append(lax.ppermute(blocks[-1], axis, right))  124 us
    psum x1, blocking collectives, shards(): totals = lax.psum(keep_flags.astype(jnp.float32), 'dp').astype(jnp.int32)  35.5 us
    unnamed x2, blocking collectives  20.6 us
    unnamed x30, local copies, waits for them, and re-layouts  11 us
    scatter x1, local copies, waits for them, and re-layouts, send_to_owners(): jnp.zeros((row_count, width), rows.dtype).at[targets]  8.27 us
    scatter x1, other arithmetic, send_to_owners(): jnp.zeros((axis_size * capacity, width), rows.dtype).at[slots]  7.39 us
    dot_general x1, matrix products, project(): jnp.dot(pooled_attended, piece.astype(jnp.float32), precision=lax.Precisi...  6.64 us
    all_to_all x1, starting transfers between devices, send_to_owners(): lax.all_to_all(packed_keys.reshape(axis_size, capacity), 'dp', split_axis...  6.31 us
  transfers between devices with their start and end apart: 18, of which 14 were waited for; matrix products, arithmetic and copies ran while one was open for 22% of the time, Pallas kernels for 0%

profile of v1, /device:TPU:0, one launch (start us, length us, event | category | flops | bytes accessed | tf_op | source)
XLA Modules:
  0.0 289.5 jit_solution(12651303037784239077)
XLA Ops:
  8.6 35.5 %psum.7 = f32[4]{0:T(128)S(1)} all-reduce(f32[4]{0:T(128)S(1)} %convert_element_type.46), channel_id=1, replica_groups=mesh['groups'=2,'dp'=16] {'dp'}, use_global_device_ids=true, to_apply=%region_0.1 | all-reduce | flops 4 | bytes 32 | tf_op jit(solution)/shard_map/psum | solution.py:129
  46.9 8.3 %all-reduce = s32[64]{0:T(128)S(1)} all-reduce(s32[64]{0:T(128)S(1)} %dynamic-update-slice), channel_id=2, replica_groups=mesh['groups'=2,'dp'=16] {'dp'}, use_global_device_ids=true, to_apply=%add | all-reduce | flops 64 | bytes 512
  56.1 2.3 gather_fusion.1
  62.8 4.5 %gather_fusion.2 = s32[512]{0:T(512)S(1)} fusion(s32[512,16]{0,1:T(8,128)S(1)} %bitcast_bitcast_fusion, s32[512]{0:T(512)S(1)} %bitcast.111), kind=kCustom, calls=%fused_computation.2 | custom fusion | bytes 8192 | tf_op jit(solution)/shard_map/jit(take_along_axis)/gather | solution.py:93
  67.3 2.4 scatter_custom_fusion
  70.5 6.3 %all-to-all-start = ((s32[16,1,48]{2,1,0:T(1,128)}), s32[16,1,48]{2,1,0:T(1,128)S(1)}, u32[]{:S(2)}, u32[]{:S(2)}) async-start(s32[16,1,48]{2,1,0:T(1,128)} %all_to_all.9), calls=%async_computation | async-start | bytes 16384 | tf_op jit(solution)/shard_map/all_to_all | solution.py:107
  77.8 3.3 %reshape.438 = bf16[4,128,4,4,128]{4,3,2,1,0:T(4,128)(2,1)S(1)} reshape(bf16[4,128,2048]{2,1,0:T(8,128)(2,1)} %param.10) | data formatting | bytes 4194304 | tf_op jit(solution)/shard_map/reshape | solution.py:53
  85.2 2.9 %copy.32 = bf16[4,128,4,4,128]{4,3,2,1,0:T(4,128)(2,1)} copy(bf16[4,128,4,4,128]{1,4,3,2,0:T(8,128)(2,1)S(1)} %bitcast.113) | data formatting | bytes 4194304 | tf_op jit(solution)/shard_map/convert_element_type | solution.py:67
  88.1 3.3 %convert_element_type.57 = bf16[512,2048]{1,0:T(8,128)(2,1)S(1)} reshape(bf16[4,128,4,4,128]{4,3,2,1,0:T(4,128)(2,1)} %copy.32) | data formatting | bytes 4194304 | tf_op jit(solution)/shard_map/convert_element_type | solution.py:67
  91.6 12.3 %all-reduce.1 = s32[64]{0:T(128)S(1)} all-reduce(s32[64]{0:T(128)S(1)} %dynamic-update-slice.1), channel_id=1, replica_groups=mesh['groups'=2,'dp'=16] {'dp'}, use_global_device_ids=true, to_apply=%add.1 | all-reduce | flops 64 | bytes 512
  105.8 3.9 %scatter_custom_fusion.3 = s32[512]{0:T(512)} fusion(s32[768]{0:T(1024)S(1)} %fusion.27, s32[768]{0:T(1024)S(1)} %reshape.499, s32[]{:T(128)} %constant.41.clone.1), kind=kCustom, calls=%fused_computation.93 | custom fusion | bytes 2052 | tf_op jit(solution)/shard_map/scatter | solution.py:117
  109.8 6.6 %multiply_reduce_fusion.1 = (f32[4]{0:T(128)S(1)}, f32[4,2048]{1,0:T(4,128)S(1)}) fusion(bf16[2048,2048]{1,0:T(8,128)(2,1)} %all-gather.3.cloned.1.call-done, f32[4,1,2048]{2,1,0:T(1,128)S(1)} %fusion.25, f32[4]{0:T(128)S(1)} %convert_reduce_fusion.1), kind=kOutput, calls=%fused_computation.57 | convolution fusion | flops 201351168 | bytes 8454176 | tf_op jit(solution)/shard_map/dot_general | solution.py:81
  117.1 6.1 %multiply_reduce_fusion = (f32[512]{0:T(512)S(1)}, f32[512,2048]{1,0:T(8,128)}) fusion(bf16[512,2048]{1,0:T(8,128)(2,1)S(1)} %convert_element_type.57, bf16[2048,2048]{1,0:T(8,128)(2,1)S(1)} %copy-done.1), kind=kOutput, calls=%fused_computation.14 | convolution fusion | flops 4297063936 | bytes 14682112 | tf_op jit(solution)/shard_map/dot_general | solution.py:80
  123.3 7.4 %scatter_custom_fusion.1 = bf16[768,2048]{1,0:T(8,128)(2,1)} fusion(s32[512]{0:T(512)S(1)} %bitcast.123, f32[512,2048]{1,0:T(8,128)} %get-tuple-element.47, f32[512]{0:T(512)S(1)} %add_rsqrt_fusion, bf16[]{:T(256)} %constant.56.clone.1), kind=kCustom, calls=%fused_computation.19 | custom fusion | flops 2097152 | bytes 7342082 | tf_op jit(solution)/shard_map/scatter | solution.py:95
  130.7 5.8 %all-to-all-start.1 = ((bf16[16,48,2048]{2,1,0:T(8,128)(2,1)}), bf16[16,48,2048]{2,1,0:T(8,128)(2,1)S(1)}, u32[]{:S(2)}, u32[]{:S(2)}) async-start(bf16[16,48,2048]{2,1,0:T(8,128)(2,1)} %bitcast.40), calls=%async_computation.1 | async-start | bytes 6291456 | tf_op jit(solution)/shard_map/all_to_all | solution.py:100
  137.6 55.5 %collective-permute-done.1 = bf16[4,2048]{1,0:T(4,128)(2,1)S(1)} collective-permute-done((bf16[4,2048]{1,0:T(4,128)(2,1)S(1)}, bf16[4,2048]{1,0:T(4,128)(2,1)S(1)}, u32[]{:S(2)}, u32[]{:S(2)}) %collective-permute-start.1) | collective-permute-done | bytes 16416 | tf_op jit(solution)/shard_map/ppermute | solution.py:21
  193.7 5.3 %collective-permute-done.2 = bf16[4,2048]{1,0:T(4,128)(2,1)S(1)} collective-permute-done((bf16[4,2048]{1,0:T(4,128)(2,1)S(1)}, bf16[4,2048]{1,0:T(4,128)(2,1)S(1)}, u32[]{:S(2)}, u32[]{:S(2)}) %collective-permute-start.2) | collective-permute-done | bytes 16416 | tf_op jit(solution)/shard_map/ppermute | solution.py:21
  199.7 5.3 %collective-permute-done.3 = bf16[4,2048]{1,0:T(4,128)(2,1)S(1)} collective-permute-done((bf16[4,2048]{1,0:T(4,128)(2,1)S(1)}, bf16[4,2048]{1,0:T(4,128)(2,1)S(1)}, u32[]{:S(2)}, u32[]{:S(2)}) %collective-permute-start.3) | collective-permute-done | bytes 16416 | tf_op jit(solution)/shard_map/ppermute | solution.py:21
  205.6 5.2 %collective-permute-done.4 = bf16[4,2048]{1,0:T(4,128)(2,1)S(1)} collective-permute-done((bf16[4,2048]{1,0:T(4,128)(2,1)S(1)}, bf16[4,2048]{1,0:T(4,128)(2,1)S(1)}, u32[]{:S(2)}, u32[]{:S(2)}) %collective-permute-start.4) | collective-permute-done | bytes 16416 | tf_op jit(solution)/shard_map/ppermute | solution.py:21
  211.5 5.2 %collective-permute-done.5 = bf16[4,2048]{1,0:T(4,128)(2,1)S(1)} collective-permute-done((bf16[4,2048]{1,0:T(4,128)(2,1)S(1)}, bf16[4,2048]{1,0:T(4,128)(2,1)S(1)}, u32[]{:S(2)}, u32[]{:S(2)}) %collective-permute-start.5) | collective-permute-done | bytes 16416 | tf_op jit(solution)/shard_map/ppermute | solution.py:21
  217.3 5.2 %collective-permute-done.6 = bf16[4,2048]{1,0:T(4,128)(2,1)S(1)} collective-permute-done((bf16[4,2048]{1,0:T(4,128)(2,1)S(1)}, bf16[4,2048]{1,0:T(4,128)(2,1)S(1)}, u32[]{:S(2)}, u32[]{:S(2)}) %collective-permute-start.6) | collective-permute-done | bytes 16416 | tf_op jit(solution)/shard_map/ppermute | solution.py:21
  223.2 5.2 %collective-permute-done.7 = bf16[4,2048]{1,0:T(4,128)(2,1)S(1)} collective-permute-done((bf16[4,2048]{1,0:T(4,128)(2,1)S(1)}, bf16[4,2048]{1,0:T(4,128)(2,1)S(1)}, u32[]{:S(2)}, u32[]{:S(2)}) %collective-permute-start.7) | collective-permute-done | bytes 16416 | tf_op jit(solution)/shard_map/ppermute | solution.py:21
  229.1 5.2 %collective-permute-done.8 = bf16[4,2048]{1,0:T(4,128)(2,1)S(1)} collective-permute-done((bf16[4,2048]{1,0:T(4,128)(2,1)S(1)}, bf16[4,2048]{1,0:T(4,128)(2,1)S(1)}, u32[]{:S(2)}, u32[]{:S(2)}) %collective-permute-start.8) | collective-permute-done | bytes 16416 | tf_op jit(solution)/shard_map/ppermute | solution.py:21
  234.9 5.2 %collective-permute-done.9 = bf16[4,2048]{1,0:T(4,128)(2,1)S(1)} collective-permute-done((bf16[4,2048]{1,0:T(4,128)(2,1)S(1)}, bf16[4,2048]{1,0:T(4,128)(2,1)S(1)}, u32[]{:S(2)}, u32[]{:S(2)}) %collective-permute-start.9) | collective-permute-done | bytes 16416 | tf_op jit(solution)/shard_map/ppermute | solution.py:21
  240.8 5.2 %collective-permute-done.10 = bf16[4,2048]{1,0:T(4,128)(2,1)S(1)} collective-permute-done((bf16[4,2048]{1,0:T(4,128)(2,1)S(1)}, bf16[4,2048]{1,0:T(4,128)(2,1)S(1)}, u32[]{:S(2)}, u32[]{:S(2)}) %collective-permute-start.10) | collective-permute-done | bytes 16416 | tf_op jit(solution)/shard_map/ppermute | solution.py:21
  246.7 5.2 %collective-permute-done.11 = bf16[4,2048]{1,0:T(4,128)(2,1)S(1)} collective-permute-done((bf16[4,2048]{1,0:T(4,128)(2,1)S(1)}, bf16[4,2048]{1,0:T(4,128)(2,1)S(1)}, u32[]{:S(2)}, u32[]{:S(2)}) %collective-permute-start.11) | collective-permute-done | bytes 16416 | tf_op jit(solution)/shard_map/ppermute | solution.py:21
  252.5 5.2 %collective-permute-done.12 = bf16[4,2048]{1,0:T(4,128)(2,1)S(1)} collective-permute-done((bf16[4,2048]{1,0:T(4,128)(2,1)S(1)}, bf16[4,2048]{1,0:T(4,128)(2,1)S(1)}, u32[]{:S(2)}, u32[]{:S(2)}) %collective-permute-start.12) | collective-permute-done | bytes 16416 | tf_op jit(solution)/shard_map/ppermute | solution.py:21
  258.4 5.2 %collective-permute-done.13 = bf16[4,2048]{1,0:T(4,128)(2,1)S(1)} collective-permute-done((bf16[4,2048]{1,0:T(4,128)(2,1)S(1)}, bf16[4,2048]{1,0:T(4,128)(2,1)S(1)}, u32[]{:S(2)}, u32[]{:S(2)}) %collective-permute-start.13) | collective-permute-done | bytes 16416 | tf_op jit(solution)/shard_map/ppermute | solution.py:21
  264.2 5.2 %collective-permute-done.14 = bf16[4,2048]{1,0:T(4,128)(2,1)S(1)} collective-permute-done((bf16[4,2048]{1,0:T(4,128)(2,1)S(1)}, bf16[4,2048]{1,0:T(4,128)(2,1)S(1)}, u32[]{:S(2)}, u32[]{:S(2)}) %collective-permute-start.14) | collective-permute-done | bytes 16416 | tf_op jit(solution)/shard_map/ppermute | solution.py:21
  270.1 1.7 gather_fusion
  272.6 1.8 convolution_convert_fusion
  274.4 8.3 %scatter_custom_fusion.2 = bf16[512,2048]{1,0:T(8,128)(2,1)} fusion(s32[768]{0:T(1024)S(1)} %fusion.27, bf16[768,2048]{1,0:T(8,128)(2,1)S(1)} %bitcast.114, bf16[]{:T(256)} %constant.56.clone.1), kind=kCustom, calls=%fused_computation.29 | custom fusion | bytes 2097154 | tf_op jit(solution)/shard_map/scatter | solution.py:116
  (97 shorter events, 27.8 us)
Async XLA Ops:
  7.2 49.0 %copy-start = (s32[1024]{0:T(1024)S(1)}, s32[1024]{0:T(1024)}, u32[]{:S(2)}) copy-start(s32[1024]{0:T(1024)} %param.17) | copy-start | bytes 12292
  7.2 69.6 %copy-start.2 = (bf16[4,128,512]{2,1,0:T(8,128)(2,1)S(1)}, bf16[4,128,512]{2,1,0:T(8,128)(2,1)}, u32[]{:S(2)}) copy-start(bf16[4,128,512]{2,1,0:T(8,128)(2,1)} %param.12) | copy-start | bytes 1572868
  7.2 102.6 %all-gather.3.cloned.1.call-start = ((), (), s32[]{:S(2)}) async-start(), calls=%async_computation.2 | async-start | bytes 8912896 | tf_op jit(solution)/shard_map/all_gather | solution.py:79
  67.3 13.8 %copy-start.3 = (bf16[4,128,512]{2,1,0:T(8,128)(2,1)S(1)}, bf16[4,128,512]{2,1,0:T(8,128)(2,1)}, u32[]{:S(2)}) copy-start(bf16[4,128,512]{2,1,0:T(8,128)(2,1)} %param.11) | copy-start | bytes 1572868
  70.5 33.5 %all-to-all-start = ((s32[16,1,48]{2,1,0:T(1,128)}), s32[16,1,48]{2,1,0:T(1,128)S(1)}, u32[]{:S(2)}, u32[]{:S(2)}) async-start(s32[16,1,48]{2,1,0:T(1,128)} %all_to_all.9), calls=%async_computation | async-start | bytes 16384 | tf_op jit(solution)/shard_map/all_to_all | solution.py:107
  82.1 1.7 copy-start.4
  109.8 7.4 %copy-start.1 = (bf16[2048,2048]{1,0:T(8,128)(2,1)S(1)}, bf16[2048,2048]{1,0:T(8,128)(2,1)}, u32[]{:S(2)}) copy-start(bf16[2048,2048]{1,0:T(8,128)(2,1)} %all-gather.3.cloned.1.call-done) | copy-start | bytes 25165828
  117.1 19.4 %collective-permute-start = (bf16[4,2048]{1,0:T(4,128)(2,1)S(1)}, bf16[4,2048]{1,0:T(4,128)(2,1)S(1)}, u32[]{:S(2)}, u32[]{:S(2)}) collective-permute-start(bf16[4,2048]{1,0:T(4,128)(2,1)S(1)} %get-tuple-element.41), channel_id=1, source_target_pairs={{0,1},{1,2},{2,3},{3,4},{4,5},{5,6},{6,7},{7,8},{8,9},{9,10},{10,1... | collective-permute-start | bytes 49160 | tf_op jit(solution)/shard_map/ppermute | solution.py:21
  130.7 143.7 %all-to-all-start.1 = ((bf16[16,48,2048]{2,1,0:T(8,128)(2,1)}), bf16[16,48,2048]{2,1,0:T(8,128)(2,1)S(1)}, u32[]{:S(2)}, u32[]{:S(2)}) async-start(bf16[16,48,2048]{2,1,0:T(8,128)(2,1)} %bitcast.40), calls=%async_computation.1 | async-start | bytes 6291456 | tf_op jit(solution)/shard_map/all_to_all | solution.py:100
  136.5 56.6 %collective-permute-start.1 = (bf16[4,2048]{1,0:T(4,128)(2,1)S(1)}, bf16[4,2048]{1,0:T(4,128)(2,1)S(1)}, u32[]{:S(2)}, u32[]{:S(2)}) collective-permute-start(bf16[4,2048]{1,0:T(4,128)(2,1)S(1)} %collective-permute-done), channel_id=1, source_target_pairs={{0,1},{1,2},{2,3},{3,4},{4,5},{5,6},{6,7},{7,8},{8,9},{9,10},{10,1... | collective-permute-start | bytes 49160 | tf_op jit(solution)/shard_map/ppermute | solution.py:21
  193.1 6.0 %collective-permute-start.2 = (bf16[4,2048]{1,0:T(4,128)(2,1)S(1)}, bf16[4,2048]{1,0:T(4,128)(2,1)S(1)}, u32[]{:S(2)}, u32[]{:S(2)}) collective-permute-start(bf16[4,2048]{1,0:T(4,128)(2,1)S(1)} %collective-permute-done.1), channel_id=1, source_target_pairs={{0,1},{1,2},{2,3},{3,4},{4,5},{5,6},{6,7},{7,8},{8,9},{9,10},{10,1... | collective-permute-start | bytes 49160 | tf_op jit(solution)/shard_map/ppermute | solution.py:21
  199.0 6.0 %collective-permute-start.3 = (bf16[4,2048]{1,0:T(4,128)(2,1)S(1)}, bf16[4,2048]{1,0:T(4,128)(2,1)S(1)}, u32[]{:S(2)}, u32[]{:S(2)}) collective-permute-start(bf16[4,2048]{1,0:T(4,128)(2,1)S(1)} %collective-permute-done.2), channel_id=1, source_target_pairs={{0,1},{1,2},{2,3},{3,4},{4,5},{5,6},{6,7},{7,8},{8,9},{9,10},{10,1... | collective-permute-start | bytes 49160 | tf_op jit(solution)/shard_map/ppermute | solution.py:21
  205.0 5.9 %collective-permute-start.4 = (bf16[4,2048]{1,0:T(4,128)(2,1)S(1)}, bf16[4,2048]{1,0:T(4,128)(2,1)S(1)}, u32[]{:S(2)}, u32[]{:S(2)}) collective-permute-start(bf16[4,2048]{1,0:T(4,128)(2,1)S(1)} %collective-permute-done.3), channel_id=1, source_target_pairs={{0,1},{1,2},{2,3},{3,4},{4,5},{5,6},{6,7},{7,8},{8,9},{9,10},{10,1... | collective-permute-start | bytes 49160 | tf_op jit(solution)/shard_map/ppermute | solution.py:21
  210.9 5.9 %collective-permute-start.5 = (bf16[4,2048]{1,0:T(4,128)(2,1)S(1)}, bf16[4,2048]{1,0:T(4,128)(2,1)S(1)}, u32[]{:S(2)}, u32[]{:S(2)}) collective-permute-start(bf16[4,2048]{1,0:T(4,128)(2,1)S(1)} %collective-permute-done.4), channel_id=1, source_target_pairs={{0,1},{1,2},{2,3},{3,4},{4,5},{5,6},{6,7},{7,8},{8,9},{9,10},{10,1... | collective-permute-start | bytes 49160 | tf_op jit(solution)/shard_map/ppermute | solution.py:21
  216.7 5.9 %collective-permute-start.6 = (bf16[4,2048]{1,0:T(4,128)(2,1)S(1)}, bf16[4,2048]{1,0:T(4,128)(2,1)S(1)}, u32[]{:S(2)}, u32[]{:S(2)}) collective-permute-start(bf16[4,2048]{1,0:T(4,128)(2,1)S(1)} %collective-permute-done.5), channel_id=1, source_target_pairs={{0,1},{1,2},{2,3},{3,4},{4,5},{5,6},{6,7},{7,8},{8,9},{9,10},{10,1... | collective-permute-start | bytes 49160 | tf_op jit(solution)/shard_map/ppermute | solution.py:21
  222.6 5.9 %collective-permute-start.7 = (bf16[4,2048]{1,0:T(4,128)(2,1)S(1)}, bf16[4,2048]{1,0:T(4,128)(2,1)S(1)}, u32[]{:S(2)}, u32[]{:S(2)}) collective-permute-start(bf16[4,2048]{1,0:T(4,128)(2,1)S(1)} %collective-permute-done.6), channel_id=1, source_target_pairs={{0,1},{1,2},{2,3},{3,4},{4,5},{5,6},{6,7},{7,8},{8,9},{9,10},{10,1... | collective-permute-start | bytes 49160 | tf_op jit(solution)/shard_map/ppermute | solution.py:21
  228.5 5.9 %collective-permute-start.8 = (bf16[4,2048]{1,0:T(4,128)(2,1)S(1)}, bf16[4,2048]{1,0:T(4,128)(2,1)S(1)}, u32[]{:S(2)}, u32[]{:S(2)}) collective-permute-start(bf16[4,2048]{1,0:T(4,128)(2,1)S(1)} %collective-permute-done.7), channel_id=1, source_target_pairs={{0,1},{1,2},{2,3},{3,4},{4,5},{5,6},{6,7},{7,8},{8,9},{9,10},{10,1... | collective-permute-start | bytes 49160 | tf_op jit(solution)/shard_map/ppermute | solution.py:21
  234.3 5.9 %collective-permute-start.9 = (bf16[4,2048]{1,0:T(4,128)(2,1)S(1)}, bf16[4,2048]{1,0:T(4,128)(2,1)S(1)}, u32[]{:S(2)}, u32[]{:S(2)}) collective-permute-start(bf16[4,2048]{1,0:T(4,128)(2,1)S(1)} %collective-permute-done.8), channel_id=1, source_target_pairs={{0,1},{1,2},{2,3},{3,4},{4,5},{5,6},{6,7},{7,8},{8,9},{9,10},{10,1... | collective-permute-start | bytes 49160 | tf_op jit(solution)/shard_map/ppermute | solution.py:21
  240.2 5.9 %collective-permute-start.10 = (bf16[4,2048]{1,0:T(4,128)(2,1)S(1)}, bf16[4,2048]{1,0:T(4,128)(2,1)S(1)}, u32[]{:S(2)}, u32[]{:S(2)}) collective-permute-start(bf16[4,2048]{1,0:T(4,128)(2,1)S(1)} %collective-permute-done.9), channel_id=1, source_target_pairs={{0,1},{1,2},{2,3},{3,4},{4,5},{5,6},{6,7},{7,8},{8,9},{9,10},{10,1... | collective-permute-start | bytes 49160 | tf_op jit(solution)/shard_map/ppermute | solution.py:21
  246.0 5.9 %collective-permute-start.11 = (bf16[4,2048]{1,0:T(4,128)(2,1)S(1)}, bf16[4,2048]{1,0:T(4,128)(2,1)S(1)}, u32[]{:S(2)}, u32[]{:S(2)}) collective-permute-start(bf16[4,2048]{1,0:T(4,128)(2,1)S(1)} %collective-permute-done.10), channel_id=1, source_target_pairs={{0,1},{1,2},{2,3},{3,4},{4,5},{5,6},{6,7},{7,8},{8,9},{9,10},{10,1... | collective-permute-start | bytes 49160 | tf_op jit(solution)/shard_map/ppermute | solution.py:21
  251.9 5.9 %collective-permute-start.12 = (bf16[4,2048]{1,0:T(4,128)(2,1)S(1)}, bf16[4,2048]{1,0:T(4,128)(2,1)S(1)}, u32[]{:S(2)}, u32[]{:S(2)}) collective-permute-start(bf16[4,2048]{1,0:T(4,128)(2,1)S(1)} %collective-permute-done.11), channel_id=1, source_target_pairs={{0,1},{1,2},{2,3},{3,4},{4,5},{5,6},{6,7},{7,8},{8,9},{9,10},{10,1... | collective-permute-start | bytes 49160 | tf_op jit(solution)/shard_map/ppermute | solution.py:21
  257.8 5.9 %collective-permute-start.13 = (bf16[4,2048]{1,0:T(4,128)(2,1)S(1)}, bf16[4,2048]{1,0:T(4,128)(2,1)S(1)}, u32[]{:S(2)}, u32[]{:S(2)}) collective-permute-start(bf16[4,2048]{1,0:T(4,128)(2,1)S(1)} %collective-permute-done.12), channel_id=1, source_target_pairs={{0,1},{1,2},{2,3},{3,4},{4,5},{5,6},{6,7},{7,8},{8,9},{9,10},{10,1... | collective-permute-start | bytes 49160 | tf_op jit(solution)/shard_map/ppermute | solution.py:21
  263.6 5.9 %collective-permute-start.14 = (bf16[4,2048]{1,0:T(4,128)(2,1)S(1)}, bf16[4,2048]{1,0:T(4,128)(2,1)S(1)}, u32[]{:S(2)}, u32[]{:S(2)}) collective-permute-start(bf16[4,2048]{1,0:T(4,128)(2,1)S(1)} %collective-permute-done.13), channel_id=1, source_target_pairs={{0,1},{1,2},{2,3},{3,4},{4,5},{5,6},{6,7},{7,8},{8,9},{9,10},{10,1... | collective-permute-start | bytes 49160 | tf_op jit(solution)/shard_map/ppermute | solution.py:21
Sparse Core Ops, SparseCore 0:
  10.2 78.0 all-gather.2
